TPU v7x, 512 devices: a whole 4x4x16 slice. The times are simulated.
512 devices in a mesh: dp: 8 (over z_hi, core), seq: 64 (over x, y, z_lo).
Axes of the slice: x: 4, y: 4, z: 16 (z_hi: 4, z_lo: 4; z = z_hi * 4 + z_lo), core: 2. Of those that a mesh axis runs over, the one named last changes fastest.
Arguments:
- first_gate: bfloat16 [8, 1024, 8192], P('dp', None, 'seq'), may hold values from -6 to 6
- second_gate: bfloat16 [8, 1024, 8192], P('dp', None, 'seq'), may hold values from -6 to 6
- value_proj: bfloat16 [8, 1024, 8192], P('dp', None, 'seq'), may hold values from -6 to 6
- grad_out: bfloat16 [8, 1024, 8192], P('dp', None, 'seq'), may hold values from -120 to 120
- filter_taps: float32 [64, 8192], P('seq'), may hold values from -1.5 to 1.5
- skip_bias: float32 [1024], replicated, may hold values from -1 to 1
Outputs:
- grad_first: bfloat16 [8, 1024, 8192], P('dp', None, 'seq')
- grad_second: bfloat16 [8, 1024, 8192], P('dp', None, 'seq')
- grad_value: bfloat16 [8, 1024, 8192], P('dp', None, 'seq')
- grad_filter: float32 [64, 8192], P('seq')
- grad_bias: float32 [1024], P('seq')
All inputs are finite; a program needn't handle non-finite values.
Results may differ from a plain program's by a relative error of at most 0.019.
Values may be sent and summed in bfloat16 or wider, within the bound.
No kernel may reach another device: no remote copies, remote signals or barrier semaphores. Data moves between devices by JAX's collectives and lax.ppermute only.
A program may use at most 64 MiB of HBM per device.

v0:
```python
import functools

import jax
import jax.numpy as jnp
from jax import lax
from jax.experimental import pallas as pl
from jax.experimental.pallas import tpu as pltpu
from jax.sharding import PartitionSpec as P

f32 = jnp.float32
bf16 = jnp.bfloat16
lanes = 128
block = 256
lag_group = 4
whole = pl.BlockSpec(memory_space=pltpu.VMEM)
params = pltpu.CompilerParams(vmem_limit_bytes=40 << 20)


def times(left, right):
    return (left.astype(f32) * right.astype(f32)).astype(bf16)


def gate_kernel(first_ref, second_ref, value_ref, grad_ref, out_ref):
    chans = first_ref.shape[1]
    out_ref[:, :chans] = times(first_ref[...], value_ref[...])
    out_ref[:, chans:] = times(grad_ref[...], second_ref[...])


def gate(first, second, value, grad):
    parts, chans, width = first.shape
    step = parts // 4
    spec = pl.BlockSpec((step, chans, width), lambda i: (i, 0, 0))
    return pl.pallas_call(
        gate_kernel,
        grid=(parts // step,),
        out_shape=jax.ShapeDtypeStruct((parts, 2 * chans, width), bf16),
        in_specs=[spec] * 4,
        out_specs=pl.BlockSpec((step, 2 * chans, width), lambda i: (i, 0, 0)),
        name="gate",
    )(first, second, value, grad)


def toeplitz_kernel(taps_ref, out_ref):
    length = taps_ref.shape[1]
    zero = jnp.zeros((1, lanes), f32)
    padded = jnp.concatenate([zero, taps_ref[...]], axis=1)
    rows = jnp.broadcast_to(padded, (8, length + lanes))
    rows = pltpu.roll(rows, 0, 1, stride=1, stride_axis=0)
    for top in range(0, lanes, 16):
        upper = rows if top == 0 else pltpu.roll(rows, top, 1)
        lower = pltpu.roll(rows, top + 8, 1)
        both = jnp.concatenate([upper, lower], axis=0)
        out_ref[top : top + 16, :] = both.astype(bf16)
    out_ref[:, :lanes] = jnp.zeros((lanes, lanes), bf16)


def toeplitz(taps):
    return pl.pallas_call(
        toeplitz_kernel,
        out_shape=jax.ShapeDtypeStruct((lanes, taps.shape[1] + lanes), bf16),
        in_specs=[whole],
        out_specs=whole,
        compiler_params=params,
        name="toeplitz",
    )(taps)


def conv_kernel(sig_ref, toep_ref, bias_ref, out_ref, x_ref, acc_ref):
    rows = sig_ref.shape[1]
    chans = rows // 2
    blocks = sig_ref.shape[0] // 2
    pad = lag_group - 1
    own = lax.axis_index("seq") * chans
    flat = bias_ref[...]
    at = lanes * lax.broadcasted_iota(jnp.int32, (chans,) + flat.shape, 1)
    at = at + lax.broadcasted_iota(jnp.int32, (chans,) + flat.shape, 2)
    want = own + lax.broadcasted_iota(jnp.int32, (chans,) + flat.shape, 0)
    bias = jnp.sum(jnp.where(at == want, flat[None], 0.0), axis=1)
    bias = jnp.sum(bias, axis=1, keepdims=True)
    bias = jnp.concatenate([bias, bias], axis=0)[None]
    row = lax.broadcasted_iota(jnp.int32, (block, block), 0)
    col = lax.broadcasted_iota(jnp.int32, (block, block), 1)
    flip = (row + col == block - 1).astype(f32).astype(bf16)
    x_ref[:pad] = jnp.zeros((pad,) + x_ref.shape[1:], bf16)
    pairs = sig_ref[...].reshape(blocks, 2, rows, lanes)
    x_ref[pad:, :chans, :lanes] = pairs[:, 0, :chans]
    x_ref[pad:, :chans, lanes:] = pairs[:, 1, :chans]
    wide = jnp.concatenate([pairs[:, 0, chans:], pairs[:, 1, chans:]], axis=2)
    wide = wide.reshape(blocks * chans, block)
    back = jnp.dot(wide, flip, preferred_element_type=f32).astype(bf16)
    for blk in range(blocks):
        src = (blocks - 1 - blk) * chans
        x_ref[pad + blk, chans:, :] = back[src : src + chans]
    for start in range(0, blocks, lag_group):
        count = blocks - start
        left = []
        right = []
        for lag in range(lag_group):
            seen = x_ref[pad - lag : pad - lag + count]
            left.append(seen.reshape(count * rows, block))
            at = block * (start + lag)
            right.append(toep_ref[:, at + lanes : at + lanes + block])
            right.append(toep_ref[:, at : at + block])
        prod = jnp.dot(
            jnp.concatenate(left, axis=1),
            jnp.concatenate(right, axis=0),
            preferred_element_type=f32,
        )
        if start == 0:
            acc_ref[...] = prod
        else:
            acc_ref[start * rows :, :] += prod
    vals = acc_ref[...].reshape(blocks, rows, block) + bias * x_ref[pad:].astype(f32)
    vals = vals.astype(bf16)
    wide = vals[:, chans:].reshape(blocks * chans, block)
    back = jnp.dot(wide, flip, preferred_element_type=f32).astype(bf16)
    for blk in range(blocks):
        out_ref[2 * blk, :chans] = vals[blk, :chans, :lanes]
        out_ref[2 * blk + 1, :chans] = vals[blk, :chans, lanes:]
        src = (blocks - 1 - blk) * chans
        out_ref[2 * blk, chans:] = back[src : src + chans, :lanes]
        out_ref[2 * blk + 1, chans:] = back[src : src + chans, lanes:]


def conv(signals, toep, bias):
    parts, rows, _ = signals.shape
    blocks = parts // 2
    return pl.pallas_call(
        conv_kernel,
        out_shape=jax.ShapeDtypeStruct(signals.shape, bf16),
        in_specs=[whole] * 3,
        out_specs=whole,
        scratch_shapes=[
            pltpu.VMEM((blocks + lag_group - 1, rows, block), bf16),
            pltpu.VMEM((blocks * rows, block), f32),
        ],
        compiler_params=params,
        name="conv",
    )(signals, toep, bias)


def cross_kernel(sig_ref, out_ref, w_ref, g_ref):
    chans = sig_ref.shape[1] // 2
    blocks = sig_ref.shape[0] // 2
    length = blocks * block
    half = blocks // 2
    span = half * chans
    pairs = sig_ref[...].reshape(blocks, 2, 2 * chans, lanes)
    mixed = jnp.concatenate([pairs[:, 0, :chans], pairs[:, 1, :chans]], axis=2)
    mixed = mixed.reshape(blocks * chans, block).astype(f32).T.astype(bf16)
    early = mixed[:, :span]
    both = jnp.concatenate([early, mixed[:, span:]], axis=0)
    wide = jnp.concatenate([pairs[:, 0, chans:], pairs[:, 1, chans:]], axis=2)
    w_ref[: blocks * chans] = wide.reshape(blocks * chans, block)
    w_ref[blocks * chans :] = jnp.zeros((span, block), bf16)
    for lag in range(half):
        low = lag * chans
        high = low + span
        far = jnp.dot(both, w_ref[high : high + span], preferred_element_type=f32)
        near = jnp.dot(early, w_ref[low : low + span], preferred_element_type=f32)
        near = near + far[block:]
        if lag == 0:
            row = lax.broadcasted_iota(jnp.int32, (block, block), 0)
            col = lax.broadcasted_iota(jnp.int32, (block, block), 1)
            near = jnp.where(col >= row, near, 0.0)
        g_ref[:, block * lag : block * lag + block] = near
        at = block * (half + lag)
        g_ref[:, at : at + block] = far[:block]
    size = block
    while size > 1:
        size //= 2
        moved = pltpu.roll(g_ref[size : 2 * size, :], length - size, 1)
        g_ref[:size, :] = g_ref[:size, :] + moved
    lines = length // lanes
    for line in range(lines):
        out_ref[line : line + 1, :] = g_ref[0:1, line * lanes : (line + 1) * lanes]
    prod = sig_ref[:, :chans].astype(f32) * sig_ref[:, chans:].astype(f32)
    total = jnp.sum(jnp.sum(prod, axis=0).T, axis=0, keepdims=True)
    rest = jnp.zeros((1, lanes - chans), f32)
    out_ref[lines : lines + 1, :] = jnp.concatenate([total, rest], axis=1)
    out_ref[lines + 1 :, :] = jnp.zeros((out_ref.shape[0] - lines - 1, lanes), f32)


def cross(signals):
    parts, rows, _ = signals.shape
    blocks = parts // 2
    chans = rows // 2
    return pl.pallas_call(
        cross_kernel,
        out_shape=jax.ShapeDtypeStruct((parts + 8, lanes), f32),
        in_specs=[whole],
        out_specs=whole,
        scratch_shapes=[
            pltpu.VMEM((blocks * chans * 3 // 2, block), bf16),
            pltpu.VMEM((block, blocks * block), f32),
        ],
        compiler_params=params,
        name="cross",
    )(signals)


def grads_kernel(back_ref, first_ref, value_ref, grad_ref, one_ref, two_ref, val_ref):
    chans = first_ref.shape[1]
    conv_vals = back_ref[:, :chans]
    back_vals = back_ref[:, chans:]
    one_ref[...] = times(back_vals, value_ref[...])
    two_ref[...] = times(grad_ref[...], conv_vals)
    val_ref[...] = times(back_vals, first_ref[...])


def grads(back, first, value, grad):
    parts, chans, width = first.shape
    step = parts // 4
    spec = pl.BlockSpec((step, chans, width), lambda i: (i, 0, 0))
    return pl.pallas_call(
        grads_kernel,
        grid=(parts // step,),
        out_shape=[jax.ShapeDtypeStruct(first.shape, bf16)] * 3,
        in_specs=[pl.BlockSpec((step, 2 * chans, width), lambda i: (i, 0, 0))] + [spec] * 3,
        out_specs=[spec] * 3,
        name="grads",
    )(back, first, value, grad)


def total_kernel(parts_ref, filter_ref, bias_ref):
    total = jnp.sum(parts_ref[...], axis=0)
    for line in range(filter_ref.shape[1] // lanes):
        filter_ref[:, line * lanes : (line + 1) * lanes] = total[line : line + 1]
    line = filter_ref.shape[1] // lanes
    bias_ref[...] = total[line : line + 1]


def per_device(first_gate, second_gate, value_proj, grad_out, filter_taps, skip_bias):
    ways = lax.axis_size("seq")
    chans = first_gate.shape[1] // ways
    shape = (ways, chans, lanes)
    first, second, value, grad = (
        arg.reshape(shape) for arg in (first_gate, second_gate, value_proj, grad_out)
    )
    toep = toeplitz(filter_taps)
    sent = gate(first, second, value, grad)
    signals = lax.all_to_all(sent, "seq", 0, 0, tiled=True)
    results = conv(signals, toep, skip_bias.reshape(-1, lanes))
    back = lax.all_to_all(results, "seq", 0, 0, tiled=True)
    partial = cross(signals)
    shares = lax.all_gather(partial, "dp")
    grad_filter, grad_bias = pl.pallas_call(
        total_kernel,
        out_shape=[
            jax.ShapeDtypeStruct(filter_taps.shape, f32),
            jax.ShapeDtypeStruct((1, lanes), f32),
        ],
        in_specs=[whole],
        out_specs=[whole] * 2,
        name="total",
    )(shares)
    outs = grads(back, first, value, grad)
    outs = [out.reshape(first_gate.shape) for out in outs]
    return (*outs, grad_filter, grad_bias[0, :chans])


def solution(mesh):
    return jax.shard_map(
        per_device,
        mesh=mesh,
        in_specs=(
            P("dp", None, "seq"),
            P("dp", None, "seq"),
            P("dp", None, "seq"),
            P("dp", None, "seq"),
            P("seq", None),
            P(),
        ),
        out_specs=(
            P("dp", None, "seq"),
            P("dp", None, "seq"),
            P("dp", None, "seq"),
            P("seq", None),
            P("seq"),
        ),
        check_vma=False,
    )
```

profile of v0, /device:TPU:39, one launch (start us, length us, event | category | flops | bytes accessed | tf_op | source)
XLA Modules:
  0.0 82.0 jit_solution(15750402463085740949)
XLA Ops:
  0.6 0.0 copy-start
  0.6 0.0 copy-start.1
  0.7 3.3 %gate.1 = bf16[64,32,128]{2,1,0:T(8,128)(2,1)} custom-call(bf16[64,16,128]{2,1,0:T(8,128)(2,1)} %bitcast.13, bf16[64,16,128]{2,1,0:T(8,128)(2,1)} %bitcast.19, bf16[64,16,128]{2,1,0:T(8,128)(2,1)} %bitcast.15, bf16[64,16,128]{2,1,0:T(8,128)(2,1)} %bitcast.17), custom_call_target="tpu_custom_call" | custom-call | tf_op jit(solution)/shard_map/gate/pallas_call | solution.py:33
  3.9 11.2 %all-to-all-start = ((bf16[64,32,128]{2,1,0:T(8,128)(2,1)}), bf16[64,32,128]{2,1,0:T(8,128)(2,1)S(1)}, u32[]{:S(2)}, u32[]{:S(2)}) async-start(bf16[64,32,128]{2,1,0:T(8,128)(2,1)} %gate.1), calls=%async_computation | async-start | bytes 1048576 | tf_op jit(solution)/shard_map/all_to_all | solution.py:242
  15.2 0.0 copy-done
  15.2 0.7 toeplitz.1.toep_ref
  15.9 14.2 %all-to-all-done.sig_ref = bf16[64,32,128]{2,1,0:T(8,128)(2,1)S(1)} async-done(((bf16[64,32,128]{2,1,0:T(8,128)(2,1)}), bf16[64,32,128]{2,1,0:T(8,128)(2,1)S(1)}, u32[]{:S(2)}, u32[]{:S(2)}) %all-to-all-start) | async-done | bytes 524320 | tf_op jit(solution)/shard_map/all_to_all | solution.py:242
  30.1 0.0 copy-done.1
  30.1 3.9 %conv.1 = bf16[64,32,128]{2,1,0:T(8,128)(2,1)} custom-call(bf16[64,32,128]{2,1,0:T(8,128)(2,1)S(1)} %all-to-all-done.sig_ref, bf16[128,8320]{1,0:T(8,128)(2,1)S(1)} %toeplitz.1.toep_ref, f32[8,128]{1,0:T(8,128)S(1)} %bitcast.11), custom_call_target="tpu_custom_call" | custom-call | tf_op jit(solution)/shard_map/conv/pallas_call | solution.py:128
  34.0 7.6 %all-to-all-start.1 = ((bf16[64,32,128]{2,1,0:T(8,128)(2,1)}), bf16[64,32,128]{2,1,0:T(8,128)(2,1)S(1)}, u32[]{:S(2)}, u32[]{:S(2)}) async-start(bf16[64,32,128]{2,1,0:T(8,128)(2,1)} %conv.1), calls=%async_computation.1 | async-start | bytes 1048576 | tf_op jit(solution)/shard_map/all_to_all | solution.py:244
  41.7 2.5 %cross.1 = f32[72,128]{1,0:T(8,128)S(1)} custom-call(bf16[64,32,128]{2,1,0:T(8,128)(2,1)S(1)} %all-to-all-done.sig_ref), custom_call_target="tpu_custom_call" | custom-call | tf_op jit(solution)/shard_map/cross/pallas_call | solution.py:188
  44.2 30.9 %all-gather = f32[576,128]{1,0:T(8,128)} all-gather(f32[72,128]{1,0:T(8,128)S(1)} %cross.1), channel_id=2, replica_groups=mesh['dp'=8,'seq'=64] {'dp'}, dimensions={0}, use_global_device_ids=true | all-gather | bytes 331776 | tf_op jit(solution)/shard_map/all_gather | solution.py:246
  75.1 1.6 %total.1 = (f32[1,8192]{1,0:T(1,128)}, f32[1,128]{1,0:T(1,128)}) custom-call(f32[8,72,128]{2,1,0:T(8,128)} %bitcast.12), custom_call_target="tpu_custom_call" | custom-call | tf_op jit(solution)/shard_map/total/pallas_call | solution.py:247
  76.7 1.2 %slice_bitcast_fusion = f32[16]{0:T(128)} fusion(f32[1,128]{1,0:T(1,128)} %get-tuple-element.14), kind=kLoop, calls=%fused_computation | loop fusion | bytes 128 | tf_op jit(solution)/shard_map/squeeze | solution.py:259
  77.9 0.0 all-to-all-done.1.back_ref
  77.9 0.0 copy-start.2
  77.9 0.8 copy-done.2
  78.7 3.3 %grads.1 = (bf16[64,16,128]{2,1,0:T(8,128)(2,1)}, bf16[64,16,128]{2,1,0:T(8,128)(2,1)}, bf16[64,16,128]{2,1,0:T(8,128)(2,1)}) custom-call(bf16[64,32,128]{2,1,0:T(8,128)(2,1)} %copy-done.2, bf16[64,16,128]{2,1,0:T(8,128)(2,1)} %bitcast.14, bf16[64,16,128]{2,1,0:T(8,128)(2,1)} %bitcast.16, bf16[64,16,128]{2,1,0:T(8,128)(2,1)} %bitcast.18), custom_call_target="tpu_custom_call" | custom-call | tf_op jit(solution)/shard_map/grads/pallas_call | solution.py:215
Async XLA Ops:
  0.6 14.5 %copy-start = (f32[1,8192]{1,0:T(1,128)S(1)}, f32[1,8192]{1,0:T(1,128)}, u32[]{:S(2)}) copy-start(f32[1,8192]{1,0:T(1,128)} %taps_ref.1) | copy-start | bytes 98308
  0.6 29.5 %copy-start.1 = (f32[1024]{0:T(1024)S(1)}, f32[1024]{0:T(1024)}, u32[]{:S(2)}) copy-start(f32[1024]{0:T(1024)} %param.11) | copy-start | bytes 12292
  3.9 26.2 %all-to-all-start = ((bf16[64,32,128]{2,1,0:T(8,128)(2,1)}), bf16[64,32,128]{2,1,0:T(8,128)(2,1)S(1)}, u32[]{:S(2)}, u32[]{:S(2)}) async-start(bf16[64,32,128]{2,1,0:T(8,128)(2,1)} %gate.1), calls=%async_computation | async-start | bytes 1048576 | tf_op jit(solution)/shard_map/all_to_all | solution.py:242
  34.0 43.9 %all-to-all-start.1 = ((bf16[64,32,128]{2,1,0:T(8,128)(2,1)}), bf16[64,32,128]{2,1,0:T(8,128)(2,1)S(1)}, u32[]{:S(2)}, u32[]{:S(2)}) async-start(bf16[64,32,128]{2,1,0:T(8,128)(2,1)} %conv.1), calls=%async_computation.1 | async-start | bytes 1048576 | tf_op jit(solution)/shard_map/all_to_all | solution.py:244
  77.9 0.8 copy-start.2
where the time goes:
time: 82.6 us; the launch traced here: 82 us
  blocking collectives  30.9 us (37%)
  starting transfers between devices  18.9 us (23%)
  Pallas kernels  15.4 us (19%)
  waiting for transfers between devices  14.2 us (17%)
  local copies, waits for them, and re-layouts  1.98 us (2%)
    all_gather x1, blocking collectives, per_device(): shares = lax.all_gather(partial, 'dp')  30.9 us
    all_to_all x1, waiting for transfers between devices, per_device(): signals = lax.all_to_all(sent, 'seq', 0, 0, tiled=True)  14.2 us
    all_to_all x1, starting transfers between devices, per_device(): signals = lax.all_to_all(sent, 'seq', 0, 0, tiled=True)  11.2 us
    all_to_all x1, starting transfers between devices, per_device(): back = lax.all_to_all(results, 'seq', 0, 0, tiled=True)  7.63 us
    pallas_call x1, Pallas kernels, conv(): pl.pallas_call(conv_kernel, out_shape=jax.ShapeDtypeStruct(signals.shape,...  3.92 us
    pallas_call x1, Pallas kernels, grads(): pl.pallas_call(grads_kernel, grid=(parts // step,), out_shape=[jax.ShapeD...  3.33 us
    pallas_call x1, Pallas kernels, gate(): pl.pallas_call(gate_kernel, grid=(parts // step,), out_shape=jax.ShapeDty...  3.28 us
    pallas_call x1, Pallas kernels, cross(): pl.pallas_call(cross_kernel, out_shape=jax.ShapeDtypeStruct((parts + 8, l...  2.53 us
  transfers between devices with their start and end apart: 2, of which 1 were waited for; matrix products, arithmetic and copies ran while one was open for 1% of the time, Pallas kernels for 6%

commit v1 on v0

--- a/solution.py
+++ b/solution.py
@@ -1,5 +1,3 @@
-import functools
-
 import jax
 import jax.numpy as jnp
 from jax import lax
@@ -13,29 +11,63 @@
 block = 256
 lag_group = 4
 whole = pl.BlockSpec(memory_space=pltpu.VMEM)
-params = pltpu.CompilerParams(vmem_limit_bytes=40 << 20)
+gate_steps = 8
+final_steps = 4
+params = pltpu.CompilerParams(vmem_limit_bytes=24 << 20)
 
 
 def times(left, right):
     return (left.astype(f32) * right.astype(f32)).astype(bf16)
 
 
-def gate_kernel(first_ref, second_ref, value_ref, grad_ref, out_ref):
-    chans = first_ref.shape[1]
-    out_ref[:, :chans] = times(first_ref[...], value_ref[...])
-    out_ref[:, chans:] = times(grad_ref[...], second_ref[...])
+def gate_kernel(first_in, second_in, value_in, grad_in, out_ref, *scratch):
+    first_ref, second_ref, value_ref, grad_ref, held, sems, out_sems = scratch
+    parts, chans, _ = first_in.shape
+    step = parts // gate_steps
+    pairs = (
+        (first_in, first_ref),
+        (value_in, value_ref),
+        (grad_in, grad_ref),
+        (second_in, second_ref),
+    )
+    loads = []
+    for at in range(gate_steps):
+        rows = pl.ds(at * step, step)
+        lot = []
+        for arg, (src, dst) in enumerate(pairs):
+            copy = pltpu.make_async_copy(src.at[rows], dst.at[rows], sems.at[at, arg])
+            copy.start()
+            lot.append(copy)
+        loads.append(lot)
+    stores = []
+    for at in range(gate_steps):
+        rows = pl.ds(at * step, step)
+        for copy in loads[at]:
+            copy.wait()
+        held[rows, :chans] = times(first_ref[rows], value_ref[rows])
+        held[rows, chans:] = times(grad_ref[rows], second_ref[rows])
+        copy = pltpu.make_async_copy(held.at[rows], out_ref.at[rows], out_sems.at[at])
+        copy.start()
+        stores.append(copy)
+    for copy in stores:
+        copy.wait()
 
 
 def gate(first, second, value, grad):
     parts, chans, width = first.shape
-    step = parts // 4
-    spec = pl.BlockSpec((step, chans, width), lambda i: (i, 0, 0))
+    spec = pl.BlockSpec(memory_space=pltpu.HBM)
     return pl.pallas_call(
         gate_kernel,
-        grid=(parts // step,),
         out_shape=jax.ShapeDtypeStruct((parts, 2 * chans, width), bf16),
         in_specs=[spec] * 4,
-        out_specs=pl.BlockSpec((step, 2 * chans, width), lambda i: (i, 0, 0)),
+        out_specs=spec,
+        scratch_shapes=[pltpu.VMEM(first.shape, bf16)] * 4
+        + [
+            pltpu.VMEM((parts, 2 * chans, width), bf16),
+            pltpu.SemaphoreType.DMA((gate_steps, 4)),
+            pltpu.SemaphoreType.DMA((gate_steps,)),
+        ],
+        compiler_params=pltpu.CompilerParams(vmem_limit_bytes=60 << 20),
         name="gate",
     )(first, second, value, grad)
 
@@ -199,35 +231,70 @@
     )(signals)
 
 
-def grads_kernel(back_ref, first_ref, value_ref, grad_ref, one_ref, two_ref, val_ref):
-    chans = first_ref.shape[1]
-    conv_vals = back_ref[:, :chans]
-    back_vals = back_ref[:, chans:]
-    one_ref[...] = times(back_vals, value_ref[...])
-    two_ref[...] = times(grad_ref[...], conv_vals)
-    val_ref[...] = times(back_vals, first_ref[...])
-
-
-def grads(back, first, value, grad):
-    parts, chans, width = first.shape
-    step = parts // 4
-    spec = pl.BlockSpec((step, chans, width), lambda i: (i, 0, 0))
-    return pl.pallas_call(
-        grads_kernel,
-        grid=(parts // step,),
-        out_shape=[jax.ShapeDtypeStruct(first.shape, bf16)] * 3,
-        in_specs=[pl.BlockSpec((step, 2 * chans, width), lambda i: (i, 0, 0))] + [spec] * 3,
-        out_specs=[spec] * 3,
-        name="grads",
-    )(back, first, value, grad)
-
-
-def total_kernel(parts_ref, filter_ref, bias_ref):
-    total = jnp.sum(parts_ref[...], axis=0)
-    for line in range(filter_ref.shape[1] // lanes):
-        filter_ref[:, line * lanes : (line + 1) * lanes] = total[line : line + 1]
-    line = filter_ref.shape[1] // lanes
-    bias_ref[...] = total[line : line + 1]
+def halve_kernel(pair_ref, half_ref, bias_ref):
+    lines = half_ref.shape[0]
+    core = lax.rem(lax.axis_index("dp"), 2)
+    rows = pl.ds(pl.multiple_of(core * lines, lines), lines)
+    half_ref[...] = (pair_ref[0, rows] + pair_ref[1, rows]).astype(bf16)
+    line = pl.ds(2 * lines, 1)
+    bias_ref[...] = (pair_ref[0, line] + pair_ref[1, line]).astype(bf16)
+
+
+def halve(pair, lines):
+    return pl.pallas_call(
+        halve_kernel,
+        out_shape=[
+            jax.ShapeDtypeStruct((lines, lanes), bf16),
+            jax.ShapeDtypeStruct((1, lanes), bf16),
+        ],
+        in_specs=[whole],
+        out_specs=[whole] * 2,
+        compiler_params=pltpu.CompilerParams(vmem_limit_bytes=4 << 20),
+        name="halve",
+    )(pair)
+
+
+def final_kernel(back_ref, first_ref, value_ref, grad_ref, sums_ref, bias_ref, *rest):
+    outs, filter_ref, total_ref, held, sems = rest[:3], rest[3], rest[4], rest[5:8], rest[8]
+    parts, chans, _ = first_ref.shape
+    step = parts // final_steps
+    copies = []
+    for at in range(final_steps):
+        rows = pl.ds(at * step, step)
+        back_vals = back_ref[rows, chans:]
+        held[0][rows] = times(back_vals, value_ref[rows])
+        held[1][rows] = times(grad_ref[rows], back_ref[rows, :chans])
+        held[2][rows] = times(back_vals, first_ref[rows])
+        for which in range(3):
+            copy = pltpu.make_async_copy(
+                held[which].at[rows], outs[which].at[rows], sems.at[at, which]
+            )
+            copy.start()
+            copies.append(copy)
+    sums = sums_ref[...].astype(f32)
+    for line in range(sums.shape[0]):
+        filter_ref[:, line * lanes : (line + 1) * lanes] = sums[line : line + 1]
+    total_ref[...] = bias_ref[0, : total_ref.shape[0]].astype(f32)
+    for copy in copies:
+        copy.wait()
+
+
+def final(back, first, value, grad, sums, bias):
+    chans = first.shape[1]
+    return pl.pallas_call(
+        final_kernel,
+        out_shape=[jax.ShapeDtypeStruct(first.shape, bf16)] * 3
+        + [
+            jax.ShapeDtypeStruct((1, sums.shape[0] * lanes), f32),
+            jax.ShapeDtypeStruct((chans,), f32),
+        ],
+        in_specs=[whole] * 6,
+        out_specs=[pl.BlockSpec(memory_space=pltpu.HBM)] * 3 + [whole] * 2,
+        scratch_shapes=[pltpu.VMEM(first.shape, bf16)] * 3
+        + [pltpu.SemaphoreType.DMA((final_steps, 3))],
+        compiler_params=pltpu.CompilerParams(vmem_limit_bytes=8 << 20),
+        name="final",
+    )(back, first, value, grad, sums, bias)
 
 
 def per_device(first_gate, second_gate, value_proj, grad_out, filter_taps, skip_bias):
@@ -243,20 +310,15 @@
     results = conv(signals, toep, skip_bias.reshape(-1, lanes))
     back = lax.all_to_all(results, "seq", 0, 0, tiled=True)
     partial = cross(signals)
-    shares = lax.all_gather(partial, "dp")
-    grad_filter, grad_bias = pl.pallas_call(
-        total_kernel,
-        out_shape=[
-            jax.ShapeDtypeStruct(filter_taps.shape, f32),
-            jax.ShapeDtypeStruct((1, lanes), f32),
-        ],
-        in_specs=[whole],
-        out_specs=[whole] * 2,
-        name="total",
-    )(shares)
-    outs = grads(back, first, value, grad)
-    outs = [out.reshape(first_gate.shape) for out in outs]
-    return (*outs, grad_filter, grad_bias[0, :chans])
+    ranks = lax.axis_size("dp")
+    cores = [[at, at + 1] for at in range(0, ranks, 2)]
+    chips = [list(range(core, ranks, 2)) for core in range(2)]
+    pair = lax.all_gather(partial, "dp", axis_index_groups=cores)
+    half, bias = halve(pair, filter_taps.shape[1] // lanes // 2)
+    half, bias = lax.psum((half, bias), "dp", axis_index_groups=chips)
+    sums = lax.all_gather(half, "dp", axis_index_groups=cores, tiled=True)
+    outs = final(back, first, value, grad, sums, bias)
+    return (*(out.reshape(first_gate.shape) for out in outs[:3]), *outs[3:])
 
 
 def solution(mesh):

time: 82.6 us -> 70.4 us (0.85)
  the two profiles are of different devices: /device:TPU:39 before, /device:TPU:1 now
where the time goes in v1:
time: 70.4 us; the launch traced here: 69.9 us
  blocking collectives  23.9 us (34%)
  starting transfers between devices  17.7 us (25%)
  waiting for transfers between devices  16.7 us (24%)
  Pallas kernels  10.9 us (15%)
  between operations  0.72 us (1%)
    psum x1, blocking collectives, per_device(): half, bias = lax.psum((half, bias), 'dp', axis_index_groups=chips)  17.1 us
    all_to_all x1, waiting for transfers between devices, per_device(): signals = lax.all_to_all(sent, 'seq', 0, 0, tiled=True)  16.7 us
    all_to_all x1, starting transfers between devices, per_device(): signals = lax.all_to_all(sent, 'seq', 0, 0, tiled=True)  12.6 us
    all_to_all x1, starting transfers between devices, per_device(): back = lax.all_to_all(results, 'seq', 0, 0, tiled=True)  5.17 us
    pallas_call x1, Pallas kernels, conv(): pl.pallas_call(conv_kernel, out_shape=jax.ShapeDtypeStruct(signals.shape,...  3.89 us
    all_gather x1, blocking collectives, per_device(): sums = lax.all_gather(half, 'dp', axis_index_groups=cores, tiled=True)  3.75 us
    all_gather x1, blocking collectives, per_device(): pair = lax.all_gather(partial, 'dp', axis_index_groups=cores)  3.05 us
    pallas_call x1, Pallas kernels, cross(): pl.pallas_call(cross_kernel, out_shape=jax.ShapeDtypeStruct((parts + 8, l...  2.53 us
  transfers between devices with their start and end apart: 2, of which 1 were waited for; matrix products, arithmetic and copies ran while one was open for 0% of the time, Pallas kernels for 5%

profile of v1, /device:TPU:1, one launch (start us, length us, event | category | flops | bytes accessed | tf_op | source)
XLA Modules:
  0.0 69.9 jit_solution(17957123018709370053)
XLA Ops:
  0.6 0.0 copy-start.3
  0.6 0.0 copy-start.4
  0.7 2.2 %gate.1 = bf16[64,32,128]{2,1,0:T(8,128)(2,1)} custom-call(bf16[64,16,128]{2,1,0:T(8,128)(2,1)} %bitcast.9, bf16[64,16,128]{2,1,0:T(8,128)(2,1)} %bitcast.17, bf16[64,16,128]{2,1,0:T(8,128)(2,1)} %bitcast.11, bf16[64,16,128]{2,1,0:T(8,128)(2,1)} %bitcast.13), custom_call_target="tpu_custom_call" | custom-call | tf_op jit(solution)/shard_map/gate/pallas_call | solution.py:59
  2.8 12.6 %all-to-all-start = ((bf16[64,32,128]{2,1,0:T(8,128)(2,1)}), bf16[64,32,128]{2,1,0:T(8,128)(2,1)S(1)}, u32[]{:S(2)}, u32[]{:S(2)}) async-start(bf16[64,32,128]{2,1,0:T(8,128)(2,1)} %gate.1), calls=%async_computation | async-start | bytes 1048576 | tf_op jit(solution)/shard_map/all_to_all | solution.py:309
  15.4 0.0 copy-done.3
  15.4 0.7 toeplitz.1.toep_ref
  16.1 16.7 %all-to-all-done.sig_ref = bf16[64,32,128]{2,1,0:T(8,128)(2,1)S(1)} async-done(((bf16[64,32,128]{2,1,0:T(8,128)(2,1)}), bf16[64,32,128]{2,1,0:T(8,128)(2,1)S(1)}, u32[]{:S(2)}, u32[]{:S(2)}) %all-to-all-start) | async-done | bytes 524320 | tf_op jit(solution)/shard_map/all_to_all | solution.py:309
  32.8 0.0 copy-done.4
  32.8 0.0 copy-start
  32.8 0.0 copy-start.1
  32.8 0.0 copy-start.2
  32.8 3.9 %conv.1 = bf16[64,32,128]{2,1,0:T(8,128)(2,1)} custom-call(bf16[64,32,128]{2,1,0:T(8,128)(2,1)S(1)} %all-to-all-done.sig_ref, bf16[128,8320]{1,0:T(8,128)(2,1)S(1)} %toeplitz.1.toep_ref, f32[8,128]{1,0:T(8,128)S(1)} %bitcast.16), custom_call_target="tpu_custom_call" | custom-call | tf_op jit(solution)/shard_map/conv/pallas_call | solution.py:160
  36.7 5.2 %all-to-all-start.1 = ((bf16[64,32,128]{2,1,0:T(8,128)(2,1)}), bf16[64,32,128]{2,1,0:T(8,128)(2,1)S(1)}, u32[]{:S(2)}, u32[]{:S(2)}) async-start(bf16[64,32,128]{2,1,0:T(8,128)(2,1)} %conv.1), calls=%async_computation.1 | async-start | bytes 1048576 | tf_op jit(solution)/shard_map/all_to_all | solution.py:311
  41.9 2.5 %cross.1 = f32[72,128]{1,0:T(8,128)S(1)} custom-call(bf16[64,32,128]{2,1,0:T(8,128)(2,1)S(1)} %all-to-all-done.sig_ref), custom_call_target="tpu_custom_call" | custom-call | tf_op jit(solution)/shard_map/cross/pallas_call | solution.py:220
  44.4 3.1 %all-gather = f32[144,128]{1,0:T(8,128)S(1)} all-gather(f32[72,128]{1,0:T(8,128)S(1)} %cross.1), channel_id=2, replica_groups={{0,64},{128,192},{256,320},{384,448},{1,65},{129,193},{257,321},{385,44..., dimensions={0}, use_global_device_ids=true | all-gather | bytes 110592 | tf_op jit(solution)/shard_map/all_gather | solution.py:316
  47.5 17.1 %all-reduce = (bf16[32,128]{1,0:T(8,128)(2,1)S(1)}, bf16[1,128]{1,0:T(2,128)(2,1)S(1)}) all-reduce(bf16[32,128]{1,0:T(8,128)(2,1)S(1)} %get-tuple-element.12, bf16[1,128]{1,0:T(2,128)(2,1)S(1)} %get-tuple-element.13), channel_id=1, replica_groups={{0,128,256,384},{64,192,320,448},{1,129,257,385},{65,193,321,449},{2,13..., use_global_device_ids=true, to_apply=%region_0.0 | all-reduce | flops 4224 | bytes 16896 | tf_op jit(solution)/shard_map/psum | solution.py:318
  64.6 3.7 %all_gather.11.sums_ref = bf16[64,128]{1,0:T(8,128)(2,1)S(1)} all-gather(bf16[32,128]{1,0:T(8,128)(2,1)S(1)} %get-tuple-element.19), channel_id=1, replica_groups={{0,64},{128,192},{256,320},{384,448},{1,65},{129,193},{257,321},{385,44..., dimensions={0}, use_global_device_ids=true | all-gather | bytes 24576 | tf_op jit(solution)/shard_map/all_gather | solution.py:319
  68.3 0.0 all-to-all-done.1.back_ref
  68.3 0.0 copy-done
  68.3 0.0 copy-done.1
  68.3 0.0 copy-done.2
  68.3 1.6 %final.1 = (bf16[64,16,128]{2,1,0:T(8,128)(2,1)}, bf16[64,16,128]{2,1,0:T(8,128)(2,1)}, bf16[64,16,128]{2,1,0:T(8,128)(2,1)}, f32[1,8192]{1,0:T(1,128)}, f32[16]{0:T(128)}) custom-call(bf16[64,32,128]{2,1,0:T(8,128)(2,1)S(1)} %all-to-all-done.1.back_ref, bf16[64,16,128]{2,1,0:T(8,128)(2,1)S(1)} %bitcast.10, bf16[64,16,128]{2,1,0:T(8,128)(2,1)S(1)} %bitcast.12, ...), custom_call_target="tpu_custom_call" | custom-call | tf_op jit(solution)/shard_map/final/pallas_call | solution.py:284
  (1 shorter events, 0.0 us)
Async XLA Ops:
  0.6 14.8 %copy-start.3 = (f32[1,8192]{1,0:T(1,128)S(1)}, f32[1,8192]{1,0:T(1,128)}, u32[]{:S(2)}) copy-start(f32[1,8192]{1,0:T(1,128)} %taps_ref.1) | copy-start | bytes 98308
  0.6 32.1 %copy-start.4 = (f32[1024]{0:T(1024)S(1)}, f32[1024]{0:T(1024)}, u32[]{:S(2)}) copy-start(f32[1024]{0:T(1024)} %param.11) | copy-start | bytes 12292
  2.8 30.0 %all-to-all-start = ((bf16[64,32,128]{2,1,0:T(8,128)(2,1)}), bf16[64,32,128]{2,1,0:T(8,128)(2,1)S(1)}, u32[]{:S(2)}, u32[]{:S(2)}) async-start(bf16[64,32,128]{2,1,0:T(8,128)(2,1)} %gate.1), calls=%async_computation | async-start | bytes 1048576 | tf_op jit(solution)/shard_map/all_to_all | solution.py:309
  32.8 35.5 %copy-start = (bf16[1,1024,128]{2,1,0:T(8,128)(2,1)S(1)}, bf16[1,1024,128]{2,1,0:T(8,128)(2,1)}, u32[]{:S(2)}) copy-start(bf16[1,1024,128]{2,1,0:T(8,128)(2,1)} %param.6) | copy-start | bytes 786436
  32.8 35.5 %copy-start.1 = (bf16[1,1024,128]{2,1,0:T(8,128)(2,1)S(1)}, bf16[1,1024,128]{2,1,0:T(8,128)(2,1)}, u32[]{:S(2)}) copy-start(bf16[1,1024,128]{2,1,0:T(8,128)(2,1)} %param.8) | copy-start | bytes 786436
  32.8 35.5 %copy-start.2 = (bf16[1,1024,128]{2,1,0:T(8,128)(2,1)S(1)}, bf16[1,1024,128]{2,1,0:T(8,128)(2,1)}, u32[]{:S(2)}) copy-start(bf16[1,1024,128]{2,1,0:T(8,128)(2,1)} %param.9) | copy-start | bytes 786436
  36.7 31.6 %all-to-all-start.1 = ((bf16[64,32,128]{2,1,0:T(8,128)(2,1)}), bf16[64,32,128]{2,1,0:T(8,128)(2,1)S(1)}, u32[]{:S(2)}, u32[]{:S(2)}) async-start(bf16[64,32,128]{2,1,0:T(8,128)(2,1)} %conv.1), calls=%async_computation.1 | async-start | bytes 1048576 | tf_op jit(solution)/shard_map/all_to_all | solution.py:311

commit v2 on v1

--- a/solution.py
+++ b/solution.py
@@ -10,10 +10,25 @@
 lanes = 128
 block = 256
 lag_group = 4
+mixed_order = (
+    13, 41, 12, 54, 44, 51, 37, 31, 57, 49, 53, 8, 40, 9, 5, 3,
+    23, 62, 43, 7, 46, 18, 59, 10, 19, 48, 38, 60, 11, 17, 47, 52,
+    28, 22, 55, 33, 15, 14, 61, 58, 20, 63, 34, 30, 56, 0, 6, 1,
+    42, 26, 50, 2, 39, 25, 24, 32, 16, 21, 36, 29, 35, 27, 4, 45,
+)
 whole = pl.BlockSpec(memory_space=pltpu.VMEM)
-gate_steps = 8
-final_steps = 4
+gate_steps = 1
+final_steps = 1
 params = pltpu.CompilerParams(vmem_limit_bytes=24 << 20)
+
+
+def seq_order(ways):
+    return mixed_order if ways == len(mixed_order) else tuple(range(ways))
+
+
+def slots(ways):
+    order = seq_order(ways)
+    return [order.index(which) for which in range(ways)]
 
 
 def times(left, right):
@@ -39,13 +54,17 @@
             copy.start()
             lot.append(copy)
         loads.append(lot)
+    for lot in loads:
+        for copy in lot:
+            copy.wait()
     stores = []
+    order = seq_order(parts)
     for at in range(gate_steps):
+        for slot in range(at * step, (at + 1) * step):
+            which = order[slot]
+            held[slot, :chans] = times(first_ref[which], value_ref[which])
+            held[slot, chans:] = times(grad_ref[which], second_ref[which])
         rows = pl.ds(at * step, step)
-        for copy in loads[at]:
-            copy.wait()
-        held[rows, :chans] = times(first_ref[rows], value_ref[rows])
-        held[rows, chans:] = times(grad_ref[rows], second_ref[rows])
         copy = pltpu.make_async_copy(held.at[rows], out_ref.at[rows], out_sems.at[at])
         copy.start()
         stores.append(copy)
@@ -109,49 +128,53 @@
     want = own + lax.broadcasted_iota(jnp.int32, (chans,) + flat.shape, 0)
     bias = jnp.sum(jnp.where(at == want, flat[None], 0.0), axis=1)
     bias = jnp.sum(bias, axis=1, keepdims=True)
-    bias = jnp.concatenate([bias, bias], axis=0)[None]
+    bias = bias[None, None]
     row = lax.broadcasted_iota(jnp.int32, (block, block), 0)
     col = lax.broadcasted_iota(jnp.int32, (block, block), 1)
     flip = (row + col == block - 1).astype(f32).astype(bf16)
-    x_ref[:pad] = jnp.zeros((pad,) + x_ref.shape[1:], bf16)
-    pairs = sig_ref[...].reshape(blocks, 2, rows, lanes)
-    x_ref[pad:, :chans, :lanes] = pairs[:, 0, :chans]
-    x_ref[pad:, :chans, lanes:] = pairs[:, 1, :chans]
-    wide = jnp.concatenate([pairs[:, 0, chans:], pairs[:, 1, chans:]], axis=2)
-    wide = wide.reshape(blocks * chans, block)
+    x_ref[:, :pad] = jnp.zeros((2, pad) + x_ref.shape[2:], bf16)
+    slot = slots(2 * blocks)
+    wide = []
+    for blk in range(blocks):
+        early, late = slot[2 * blk], slot[2 * blk + 1]
+        x_ref[0, pad + blk, :, :lanes] = sig_ref[early, :chans]
+        x_ref[0, pad + blk, :, lanes:] = sig_ref[late, :chans]
+        wide.append(jnp.concatenate([sig_ref[early, chans:], sig_ref[late, chans:]], axis=1))
+    wide = jnp.concatenate(wide[::-1], axis=0)
     back = jnp.dot(wide, flip, preferred_element_type=f32).astype(bf16)
-    for blk in range(blocks):
-        src = (blocks - 1 - blk) * chans
-        x_ref[pad + blk, chans:, :] = back[src : src + chans]
+    x_ref[1, pad:] = back.reshape(blocks, chans, block)
     for start in range(0, blocks, lag_group):
         count = blocks - start
-        left = []
         right = []
         for lag in range(lag_group):
-            seen = x_ref[pad - lag : pad - lag + count]
-            left.append(seen.reshape(count * rows, block))
             at = block * (start + lag)
             right.append(toep_ref[:, at + lanes : at + lanes + block])
             right.append(toep_ref[:, at : at + block])
-        prod = jnp.dot(
-            jnp.concatenate(left, axis=1),
-            jnp.concatenate(right, axis=0),
-            preferred_element_type=f32,
-        )
+        right = jnp.concatenate(right, axis=0)
+        left = []
+        for which in range(2):
+            seen = [
+                x_ref[which, pad - lag : pad - lag + count].reshape(count * chans, block)
+                for lag in range(lag_group)
+            ]
+            left.append(jnp.concatenate(seen, axis=1))
+        prod = jnp.dot(jnp.concatenate(left, axis=0), right, preferred_element_type=f32)
+        prod = prod.reshape(2, count * chans, block)
         if start == 0:
             acc_ref[...] = prod
         else:
-            acc_ref[start * rows :, :] += prod
-    vals = acc_ref[...].reshape(blocks, rows, block) + bias * x_ref[pad:].astype(f32)
-    vals = vals.astype(bf16)
-    wide = vals[:, chans:].reshape(blocks * chans, block)
+            acc_ref[:, start * chans :, :] += prod
+    sums = acc_ref[...].reshape(2, blocks, chans, block)
+    vals = (sums + bias * x_ref[:, pad:].astype(f32)).astype(bf16)
+    wide = vals[1].reshape(blocks * chans, block)
     back = jnp.dot(wide, flip, preferred_element_type=f32).astype(bf16)
     for blk in range(blocks):
-        out_ref[2 * blk, :chans] = vals[blk, :chans, :lanes]
-        out_ref[2 * blk + 1, :chans] = vals[blk, :chans, lanes:]
+        early, late = slot[2 * blk], slot[2 * blk + 1]
+        out_ref[early, :chans] = vals[0, blk, :, :lanes]
+        out_ref[late, :chans] = vals[0, blk, :, lanes:]
         src = (blocks - 1 - blk) * chans
-        out_ref[2 * blk, chans:] = back[src : src + chans, :lanes]
-        out_ref[2 * blk + 1, chans:] = back[src : src + chans, lanes:]
+        out_ref[early, chans:] = back[src : src + chans, :lanes]
+        out_ref[late, chans:] = back[src : src + chans, lanes:]
 
 
 def conv(signals, toep, bias):
@@ -163,8 +186,8 @@
         in_specs=[whole] * 3,
         out_specs=whole,
         scratch_shapes=[
-            pltpu.VMEM((blocks + lag_group - 1, rows, block), bf16),
-            pltpu.VMEM((blocks * rows, block), f32),
+            pltpu.VMEM((2, blocks + lag_group - 1, rows // 2, block), bf16),
+            pltpu.VMEM((2, blocks * rows // 2, block), f32),
         ],
         compiler_params=params,
         name="conv",
@@ -172,50 +195,47 @@
 
 
 def cross_kernel(sig_ref, out_ref, w_ref, g_ref):
-    chans = sig_ref.shape[1] // 2
-    blocks = sig_ref.shape[0] // 2
-    length = blocks * block
-    half = blocks // 2
-    span = half * chans
-    pairs = sig_ref[...].reshape(blocks, 2, 2 * chans, lanes)
-    mixed = jnp.concatenate([pairs[:, 0, :chans], pairs[:, 1, :chans]], axis=2)
-    mixed = mixed.reshape(blocks * chans, block).astype(f32).T.astype(bf16)
-    early = mixed[:, :span]
-    both = jnp.concatenate([early, mixed[:, span:]], axis=0)
-    wide = jnp.concatenate([pairs[:, 0, chans:], pairs[:, 1, chans:]], axis=2)
-    w_ref[: blocks * chans] = wide.reshape(blocks * chans, block)
-    w_ref[blocks * chans :] = jnp.zeros((span, block), bf16)
-    for lag in range(half):
+    parts, rows, _ = sig_ref.shape
+    chans = rows // 2
+    length = parts * lanes
+    slot = slots(parts)
+    mixed = jnp.concatenate([sig_ref[slot[one], :chans] for one in range(parts)], axis=0)
+    mixed = mixed.astype(f32).T.astype(bf16)
+    for one in range(parts):
+        part = sig_ref[slot[one], chans:]
+        w_ref[one * chans : (one + 1) * chans, :lanes] = part
+        if one:
+            w_ref[(one - 1) * chans : one * chans, lanes:] = part
+    w_ref[(parts - 1) * chans : parts * chans, lanes:] = jnp.zeros((chans, lanes), bf16)
+    over = w_ref.shape[0] - parts * chans
+    w_ref[parts * chans :] = jnp.zeros((over, block), bf16)
+    for lag in range(0, parts, 2):
+        depth = -(-(parts - lag) * chans // block) * block
         low = lag * chans
-        high = low + span
-        far = jnp.dot(both, w_ref[high : high + span], preferred_element_type=f32)
-        near = jnp.dot(early, w_ref[low : low + span], preferred_element_type=f32)
-        near = near + far[block:]
+        near = jnp.dot(
+            mixed[:, :depth], w_ref[low : low + depth], preferred_element_type=f32
+        )
         if lag == 0:
-            row = lax.broadcasted_iota(jnp.int32, (block, block), 0)
-            col = lax.broadcasted_iota(jnp.int32, (block, block), 1)
+            row = lax.broadcasted_iota(jnp.int32, near.shape, 0)
+            col = lax.broadcasted_iota(jnp.int32, near.shape, 1)
             near = jnp.where(col >= row, near, 0.0)
-        g_ref[:, block * lag : block * lag + block] = near
-        at = block * (half + lag)
-        g_ref[:, at : at + block] = far[:block]
-    size = block
+        g_ref[:, lanes * lag : lanes * lag + block] = near
+    size = lanes
     while size > 1:
         size //= 2
         moved = pltpu.roll(g_ref[size : 2 * size, :], length - size, 1)
         g_ref[:size, :] = g_ref[:size, :] + moved
-    lines = length // lanes
-    for line in range(lines):
-        out_ref[line : line + 1, :] = g_ref[0:1, line * lanes : (line + 1) * lanes]
+    for one in range(parts):
+        out_ref[one : one + 1, :] = g_ref[0:1, one * lanes : (one + 1) * lanes]
     prod = sig_ref[:, :chans].astype(f32) * sig_ref[:, chans:].astype(f32)
     total = jnp.sum(jnp.sum(prod, axis=0).T, axis=0, keepdims=True)
     rest = jnp.zeros((1, lanes - chans), f32)
-    out_ref[lines : lines + 1, :] = jnp.concatenate([total, rest], axis=1)
-    out_ref[lines + 1 :, :] = jnp.zeros((out_ref.shape[0] - lines - 1, lanes), f32)
+    out_ref[parts : parts + 1, :] = jnp.concatenate([total, rest], axis=1)
+    out_ref[parts + 1 :, :] = jnp.zeros((out_ref.shape[0] - parts - 1, lanes), f32)
 
 
 def cross(signals):
     parts, rows, _ = signals.shape
-    blocks = parts // 2
     chans = rows // 2
     return pl.pallas_call(
         cross_kernel,
@@ -223,8 +243,8 @@
         in_specs=[whole],
         out_specs=whole,
         scratch_shapes=[
-            pltpu.VMEM((blocks * chans * 3 // 2, block), bf16),
-            pltpu.VMEM((block, blocks * block), f32),
+            pltpu.VMEM((parts * chans + block, block), bf16),
+            pltpu.VMEM((lanes, parts * lanes), f32),
         ],
         compiler_params=params,
         name="cross",
@@ -255,16 +275,18 @@
 
 
 def final_kernel(back_ref, first_ref, value_ref, grad_ref, sums_ref, bias_ref, *rest):
-    outs, filter_ref, total_ref, held, sems = rest[:3], rest[3], rest[4], rest[5:8], rest[8]
+    outs, held, sems = rest[:5], rest[5:10], rest[10]
     parts, chans, _ = first_ref.shape
     step = parts // final_steps
+    slot = slots(parts)
     copies = []
     for at in range(final_steps):
+        for one in range(at * step, (at + 1) * step):
+            back_vals = back_ref[slot[one], chans:]
+            held[0][one] = times(back_vals, value_ref[one])
+            held[1][one] = times(grad_ref[one], back_ref[slot[one], :chans])
+            held[2][one] = times(back_vals, first_ref[one])
         rows = pl.ds(at * step, step)
-        back_vals = back_ref[rows, chans:]
-        held[0][rows] = times(back_vals, value_ref[rows])
-        held[1][rows] = times(grad_ref[rows], back_ref[rows, :chans])
-        held[2][rows] = times(back_vals, first_ref[rows])
         for which in range(3):
             copy = pltpu.make_async_copy(
                 held[which].at[rows], outs[which].at[rows], sems.at[at, which]
@@ -273,25 +295,27 @@
             copies.append(copy)
     sums = sums_ref[...].astype(f32)
     for line in range(sums.shape[0]):
-        filter_ref[:, line * lanes : (line + 1) * lanes] = sums[line : line + 1]
-    total_ref[...] = bias_ref[0, : total_ref.shape[0]].astype(f32)
+        held[3][:, line * lanes : (line + 1) * lanes] = sums[line : line + 1]
+    held[4][...] = bias_ref[0, :chans].astype(f32)
+    for which in (3, 4):
+        copy = pltpu.make_async_copy(held[which], outs[which], sems.at[final_steps, which - 3])
+        copy.start()
+        copies.append(copy)
     for copy in copies:
         copy.wait()
 
 
 def final(back, first, value, grad, sums, bias):
     chans = first.shape[1]
+    line = (1, sums.shape[0] * lanes)
+    shapes = [(first.shape, bf16)] * 3 + [(line, f32), ((chans,), f32)]
     return pl.pallas_call(
         final_kernel,
-        out_shape=[jax.ShapeDtypeStruct(first.shape, bf16)] * 3
-        + [
-            jax.ShapeDtypeStruct((1, sums.shape[0] * lanes), f32),
-            jax.ShapeDtypeStruct((chans,), f32),
-        ],
+        out_shape=[jax.ShapeDtypeStruct(*shape) for shape in shapes],
         in_specs=[whole] * 6,
-        out_specs=[pl.BlockSpec(memory_space=pltpu.HBM)] * 3 + [whole] * 2,
-        scratch_shapes=[pltpu.VMEM(first.shape, bf16)] * 3
-        + [pltpu.SemaphoreType.DMA((final_steps, 3))],
+        out_specs=[pl.BlockSpec(memory_space=pltpu.HBM)] * 5,
+        scratch_shapes=[pltpu.VMEM(*shape) for shape in shapes]
+        + [pltpu.SemaphoreType.DMA((final_steps + 1, 3))],
         compiler_params=pltpu.CompilerParams(vmem_limit_bytes=8 << 20),
         name="final",
     )(back, first, value, grad, sums, bias)
@@ -306,9 +330,10 @@
     )
     toep = toeplitz(filter_taps)
     sent = gate(first, second, value, grad)
-    signals = lax.all_to_all(sent, "seq", 0, 0, tiled=True)
+    order = [seq_order(ways)]
+    signals = lax.all_to_all(sent, "seq", 0, 0, axis_index_groups=order, tiled=True)
     results = conv(signals, toep, skip_bias.reshape(-1, lanes))
-    back = lax.all_to_all(results, "seq", 0, 0, tiled=True)
+    back = lax.all_to_all(results, "seq", 0, 0, axis_index_groups=order, tiled=True)
     partial = cross(signals)
     ranks = lax.axis_size("dp")
     cores = [[at, at + 1] for at in range(0, ranks, 2)]

time: 70.4 us -> 69.4 us (0.986)
  waiting for transfers between devices: 16.7 us -> 14 us
  starting transfers between devices: 17.7 us -> 19.5 us
  blocking collectives: 23.9 us -> 24.8 us
  Pallas kernels: 10.9 us -> 10 us
    all_to_all x2, waiting for transfers between devices: 16.7 us -> 14 us  [the longest x1 14 us: per_device(): lax.all_to_all(sent, 'seq', 0, 0, axis_index_groups=order, tiled=True)]
    all_to_all x2, starting transfers between devices: 17.7 us -> 19.5 us  [the longest x1 13.1 us: per_device(): lax.all_to_all(sent, 'seq', 0, 0, axis_index_groups=order, tiled=True)]
    all_gather x1, blocking collectives: 3.05 us -> 3.92 us  [per_device(): pair = lax.all_gather(partial, 'dp', axis_index_groups=cores)]
where the time goes in v2:
time: 69.4 us; the launch traced here: 69.1 us
  blocking collectives  24.8 us (36%)
  starting transfers between devices  19.5 us (28%)
  waiting for transfers between devices  14 us (20%)
  Pallas kernels  10 us (14%)
  between operations  0.72 us (1%)
    psum x1, blocking collectives, per_device(): half, bias = lax.psum((half, bias), 'dp', axis_index_groups=chips)  17.2 us
    all_to_all x1, waiting for transfers between devices, per_device(): lax.all_to_all(sent, 'seq', 0, 0, axis_index_groups=order, tiled=True)  14 us
    all_to_all x1, starting transfers between devices, per_device(): lax.all_to_all(sent, 'seq', 0, 0, axis_index_groups=order, tiled=True)  13.1 us
    all_to_all x1, starting transfers between devices, per_device(): lax.all_to_all(results, 'seq', 0, 0, axis_index_groups=order, tiled=True)  6.44 us
    all_gather x1, blocking collectives, per_device(): pair = lax.all_gather(partial, 'dp', axis_index_groups=cores)  3.92 us
    pallas_call x1, Pallas kernels, conv(): pl.pallas_call(conv_kernel, out_shape=jax.ShapeDtypeStruct(signals.shape,...  3.74 us
    all_gather x1, blocking collectives, per_device(): sums = lax.all_gather(half, 'dp', axis_index_groups=cores, tiled=True)  3.7 us
    pallas_call x1, Pallas kernels, cross(): pl.pallas_call(cross_kernel, out_shape=jax.ShapeDtypeStruct((parts + 8, l...  2.43 us
  transfers between devices with their start and end apart: 2, of which 1 were waited for; matrix products, arithmetic and copies ran while one was open for 0% of the time, Pallas kernels for 5%

profile of v2, /device:TPU:1, one launch (start us, length us, event | category | flops | bytes accessed | tf_op | source)
XLA Modules:
  0.0 69.1 jit_solution(17681270077147567037)
XLA Ops:
  0.6 0.0 copy-start.3
  0.6 0.0 copy-start.4
  0.7 2.2 %gate.1 = bf16[64,32,128]{2,1,0:T(8,128)(2,1)} custom-call(bf16[64,16,128]{2,1,0:T(8,128)(2,1)} %bitcast.9, bf16[64,16,128]{2,1,0:T(8,128)(2,1)} %bitcast.17, bf16[64,16,128]{2,1,0:T(8,128)(2,1)} %bitcast.11, bf16[64,16,128]{2,1,0:T(8,128)(2,1)} %bitcast.13), custom_call_target="tpu_custom_call" | custom-call | tf_op jit(solution)/shard_map/gate/pallas_call | solution.py:78
  2.8 13.1 %all-to-all-start = ((bf16[64,32,128]{2,1,0:T(8,128)(2,1)}), bf16[64,32,128]{2,1,0:T(8,128)(2,1)S(1)}, u32[]{:S(2)}, u32[]{:S(2)}) async-start(bf16[64,32,128]{2,1,0:T(8,128)(2,1)} %gate.1), calls=%async_computation | async-start | bytes 1048576 | tf_op jit(solution)/shard_map/all_to_all | solution.py:334
  15.9 0.0 copy-done.3
  15.9 0.7 %toeplitz.1.toep_ref = bf16[128,8320]{1,0:T(8,128)(2,1)S(1)} custom-call(f32[1,8192]{1,0:T(1,128)S(1)} %copy-done.3), custom_call_target="tpu_custom_call" | custom-call | tf_op jit(solution)/shard_map/toeplitz/pallas_call | solution.py:109
  16.6 14.0 %all-to-all-done.sig_ref = bf16[64,32,128]{2,1,0:T(8,128)(2,1)S(1)} async-done(((bf16[64,32,128]{2,1,0:T(8,128)(2,1)}), bf16[64,32,128]{2,1,0:T(8,128)(2,1)S(1)}, u32[]{:S(2)}, u32[]{:S(2)}) %all-to-all-start) | async-done | bytes 524320 | tf_op jit(solution)/shard_map/all_to_all | solution.py:334
  30.6 0.0 copy-done.4
  30.6 0.0 copy-start
  30.6 0.0 copy-start.1
  30.6 0.0 copy-start.2
  30.6 3.7 %conv.1 = bf16[64,32,128]{2,1,0:T(8,128)(2,1)} custom-call(bf16[64,32,128]{2,1,0:T(8,128)(2,1)S(1)} %all-to-all-done.sig_ref, bf16[128,8320]{1,0:T(8,128)(2,1)S(1)} %toeplitz.1.toep_ref, f32[8,128]{1,0:T(8,128)S(1)} %bitcast.16), custom_call_target="tpu_custom_call" | custom-call | tf_op jit(solution)/shard_map/conv/pallas_call | solution.py:183
  34.3 6.4 %all-to-all-start.1 = ((bf16[64,32,128]{2,1,0:T(8,128)(2,1)}), bf16[64,32,128]{2,1,0:T(8,128)(2,1)S(1)}, u32[]{:S(2)}, u32[]{:S(2)}) async-start(bf16[64,32,128]{2,1,0:T(8,128)(2,1)} %conv.1), calls=%async_computation.1 | async-start | bytes 1048576 | tf_op jit(solution)/shard_map/all_to_all | solution.py:336
  40.8 2.4 %cross.1 = f32[72,128]{1,0:T(8,128)S(1)} custom-call(bf16[64,32,128]{2,1,0:T(8,128)(2,1)S(1)} %all-to-all-done.sig_ref), custom_call_target="tpu_custom_call" | custom-call | tf_op jit(solution)/shard_map/cross/pallas_call | solution.py:240
  43.2 3.9 %all-gather = f32[144,128]{1,0:T(8,128)S(1)} all-gather(f32[72,128]{1,0:T(8,128)S(1)} %cross.1), channel_id=2, replica_groups={{0,64},{128,192},{256,320},{384,448},{1,65},{129,193},{257,321},{385,44..., dimensions={0}, use_global_device_ids=true | all-gather | bytes 110592 | tf_op jit(solution)/shard_map/all_gather | solution.py:341
  47.1 17.2 %all-reduce = (bf16[32,128]{1,0:T(8,128)(2,1)S(1)}, bf16[1,128]{1,0:T(2,128)(2,1)S(1)}) all-reduce(bf16[32,128]{1,0:T(8,128)(2,1)S(1)} %get-tuple-element.12, bf16[1,128]{1,0:T(2,128)(2,1)S(1)} %get-tuple-element.13), channel_id=1, replica_groups={{0,128,256,384},{64,192,320,448},{1,129,257,385},{65,193,321,449},{2,13..., use_global_device_ids=true, to_apply=%region_0.0 | all-reduce | flops 4224 | bytes 16896 | tf_op jit(solution)/shard_map/psum | solution.py:343
  64.4 3.7 %all_gather.11.sums_ref = bf16[64,128]{1,0:T(8,128)(2,1)S(1)} all-gather(bf16[32,128]{1,0:T(8,128)(2,1)S(1)} %get-tuple-element.19), channel_id=1, replica_groups={{0,64},{128,192},{256,320},{384,448},{1,65},{129,193},{257,321},{385,44..., dimensions={0}, use_global_device_ids=true | all-gather | bytes 24576 | tf_op jit(solution)/shard_map/all_gather | solution.py:344
  68.0 0.0 all-to-all-done.1.back_ref
  68.0 0.0 copy-done
  68.1 0.0 copy-done.1
  68.1 0.0 copy-done.2
  68.1 1.0 %final.1 = (bf16[64,16,128]{2,1,0:T(8,128)(2,1)}, bf16[64,16,128]{2,1,0:T(8,128)(2,1)}, bf16[64,16,128]{2,1,0:T(8,128)(2,1)}, f32[1,8192]{1,0:T(1,128)}, f32[16]{0:T(128)}) custom-call(bf16[64,32,128]{2,1,0:T(8,128)(2,1)S(1)} %all-to-all-done.1.back_ref, bf16[64,16,128]{2,1,0:T(8,128)(2,1)S(1)} %bitcast.10, bf16[64,16,128]{2,1,0:T(8,128)(2,1)S(1)} %bitcast.12, ...), custom_call_target="tpu_custom_call" | custom-call | tf_op jit(solution)/shard_map/final/pallas_call | solution.py:312
  (1 shorter events, 0.0 us)
Async XLA Ops:
  0.6 15.3 %copy-start.3 = (f32[1,8192]{1,0:T(1,128)S(1)}, f32[1,8192]{1,0:T(1,128)}, u32[]{:S(2)}) copy-start(f32[1,8192]{1,0:T(1,128)} %taps_ref.1) | copy-start | bytes 98308
  0.6 29.9 %copy-start.4 = (f32[1024]{0:T(1024)S(1)}, f32[1024]{0:T(1024)}, u32[]{:S(2)}) copy-start(f32[1024]{0:T(1024)} %param.11) | copy-start | bytes 12292
  2.8 27.7 %all-to-all-start = ((bf16[64,32,128]{2,1,0:T(8,128)(2,1)}), bf16[64,32,128]{2,1,0:T(8,128)(2,1)S(1)}, u32[]{:S(2)}, u32[]{:S(2)}) async-start(bf16[64,32,128]{2,1,0:T(8,128)(2,1)} %gate.1), calls=%async_computation | async-start | bytes 1048576 | tf_op jit(solution)/shard_map/all_to_all | solution.py:334
  30.6 37.5 %copy-start = (bf16[1,1024,128]{2,1,0:T(8,128)(2,1)S(1)}, bf16[1,1024,128]{2,1,0:T(8,128)(2,1)}, u32[]{:S(2)}) copy-start(bf16[1,1024,128]{2,1,0:T(8,128)(2,1)} %param.6) | copy-start | bytes 786436
  30.6 37.5 %copy-start.1 = (bf16[1,1024,128]{2,1,0:T(8,128)(2,1)S(1)}, bf16[1,1024,128]{2,1,0:T(8,128)(2,1)}, u32[]{:S(2)}) copy-start(bf16[1,1024,128]{2,1,0:T(8,128)(2,1)} %param.8) | copy-start | bytes 786436
  30.6 37.5 %copy-start.2 = (bf16[1,1024,128]{2,1,0:T(8,128)(2,1)S(1)}, bf16[1,1024,128]{2,1,0:T(8,128)(2,1)}, u32[]{:S(2)}) copy-start(bf16[1,1024,128]{2,1,0:T(8,128)(2,1)} %param.9) | copy-start | bytes 786436
  34.3 33.7 %all-to-all-start.1 = ((bf16[64,32,128]{2,1,0:T(8,128)(2,1)}), bf16[64,32,128]{2,1,0:T(8,128)(2,1)S(1)}, u32[]{:S(2)}, u32[]{:S(2)}) async-start(bf16[64,32,128]{2,1,0:T(8,128)(2,1)} %conv.1), calls=%async_computation.1 | async-start | bytes 1048576 | tf_op jit(solution)/shard_map/all_to_all | solution.py:336

commit v3 on v2

--- a/solution.py
+++ b/solution.py
@@ -11,10 +11,10 @@
 block = 256
 lag_group = 4
 mixed_order = (
-    13, 41, 12, 54, 44, 51, 37, 31, 57, 49, 53, 8, 40, 9, 5, 3,
-    23, 62, 43, 7, 46, 18, 59, 10, 19, 48, 38, 60, 11, 17, 47, 52,
-    28, 22, 55, 33, 15, 14, 61, 58, 20, 63, 34, 30, 56, 0, 6, 1,
-    42, 26, 50, 2, 39, 25, 24, 32, 16, 21, 36, 29, 35, 27, 4, 45,
+    17, 50, 1, 15, 12, 14, 30, 41, 37, 57, 60, 21, 35, 8, 61, 10,
+    22, 7, 44, 63, 46, 20, 55, 0, 31, 13, 58, 49, 19, 16, 25, 54,
+    36, 48, 52, 45, 34, 4, 26, 5, 3, 9, 51, 27, 24, 18, 38, 29,
+    43, 6, 33, 28, 23, 56, 2, 32, 40, 62, 47, 53, 42, 39, 59, 11,
 )
 whole = pl.BlockSpec(memory_space=pltpu.VMEM)
 gate_steps = 1
@@ -220,17 +220,19 @@
             col = lax.broadcasted_iota(jnp.int32, near.shape, 1)
             near = jnp.where(col >= row, near, 0.0)
         g_ref[:, lanes * lag : lanes * lag + block] = near
-    size = lanes
+    total = g_ref[:8, :]
+    for top in range(8, lanes, 8):
+        total = total + pltpu.roll(g_ref[top : top + 8, :], length - top, 1)
+    size = 8
     while size > 1:
         size //= 2
-        moved = pltpu.roll(g_ref[size : 2 * size, :], length - size, 1)
-        g_ref[:size, :] = g_ref[:size, :] + moved
+        total = total[:size] + pltpu.roll(total[size : 2 * size], length - size, 1)
     for one in range(parts):
-        out_ref[one : one + 1, :] = g_ref[0:1, one * lanes : (one + 1) * lanes]
+        out_ref[one : one + 1, :] = total[:, one * lanes : (one + 1) * lanes]
     prod = sig_ref[:, :chans].astype(f32) * sig_ref[:, chans:].astype(f32)
-    total = jnp.sum(jnp.sum(prod, axis=0).T, axis=0, keepdims=True)
+    bias = jnp.sum(jnp.sum(prod, axis=0).T, axis=0, keepdims=True)
     rest = jnp.zeros((1, lanes - chans), f32)
-    out_ref[parts : parts + 1, :] = jnp.concatenate([total, rest], axis=1)
+    out_ref[parts : parts + 1, :] = jnp.concatenate([bias, rest], axis=1)
     out_ref[parts + 1 :, :] = jnp.zeros((out_ref.shape[0] - parts - 1, lanes), f32)
 
 

time: 69.4 us -> 68.3 us (0.984)
  starting transfers between devices: 19.5 us -> 17.1 us
  waiting for transfers between devices: 14 us -> 15.7 us
    all_to_all x1, starting transfers between devices: 6.44 us -> 4.64 us  [per_device(): lax.all_to_all(results, 'seq', 0, 0, axis_index_groups=order, tiled=True)]
    all_to_all x1, waiting for transfers between devices: 14 us -> 15.7 us  [per_device(): lax.all_to_all(sent, 'seq', 0, 0, axis_index_groups=order, tiled=True)]
  transfers between devices with their start and end apart: 2 -> 2, of which waited for: 1 -> 1; matrix products, arithmetic and copies ran while one was open for 0% -> 0% of each run, Pallas kernels for 5% -> 4%
where the time goes in v3:
time: 68.3 us; the launch traced here: 67.9 us
  blocking collectives  24.5 us (36%)
  starting transfers between devices  17.1 us (25%)
  waiting for transfers between devices  15.7 us (23%)
  Pallas kernels  9.9 us (14%)
  between operations  0.72 us (1%)
    psum x1, blocking collectives, per_device(): half, bias = lax.psum((half, bias), 'dp', axis_index_groups=chips)  17.2 us
    all_to_all x1, waiting for transfers between devices, per_device(): lax.all_to_all(sent, 'seq', 0, 0, axis_index_groups=order, tiled=True)  15.7 us
    all_to_all x1, starting transfers between devices, per_device(): lax.all_to_all(sent, 'seq', 0, 0, axis_index_groups=order, tiled=True)  12.5 us
    all_to_all x1, starting transfers between devices, per_device(): lax.all_to_all(results, 'seq', 0, 0, axis_index_groups=order, tiled=True)  4.64 us
    all_gather x1, blocking collectives, per_device(): pair = lax.all_gather(partial, 'dp', axis_index_groups=cores)  3.76 us
    pallas_call x1, Pallas kernels, conv(): pl.pallas_call(conv_kernel, out_shape=jax.ShapeDtypeStruct(signals.shape,...  3.74 us
    all_gather x1, blocking collectives, per_device(): sums = lax.all_gather(half, 'dp', axis_index_groups=cores, tiled=True)  3.57 us
    pallas_call x1, Pallas kernels, cross(): pl.pallas_call(cross_kernel, out_shape=jax.ShapeDtypeStruct((parts + 8, l...  2.3 us
  transfers between devices with their start and end apart: 2, of which 1 were waited for; matrix products, arithmetic and copies ran while one was open for 0% of the time, Pallas kernels for 4%

profile of v3, /device:TPU:1, one launch (start us, length us, event | category | flops | bytes accessed | tf_op | source)
XLA Modules:
  0.0 67.9 jit_solution(15887635282133982731)
XLA Ops:
  0.6 0.0 copy-start.3
  0.6 0.0 copy-start.4
  0.7 2.2 %gate.1 = bf16[64,32,128]{2,1,0:T(8,128)(2,1)} custom-call(bf16[64,16,128]{2,1,0:T(8,128)(2,1)} %bitcast.9, bf16[64,16,128]{2,1,0:T(8,128)(2,1)} %bitcast.17, bf16[64,16,128]{2,1,0:T(8,128)(2,1)} %bitcast.11, bf16[64,16,128]{2,1,0:T(8,128)(2,1)} %bitcast.13), custom_call_target="tpu_custom_call" | custom-call | tf_op jit(solution)/shard_map/gate/pallas_call | solution.py:78
  2.8 12.5 %all-to-all-start = ((bf16[64,32,128]{2,1,0:T(8,128)(2,1)}), bf16[64,32,128]{2,1,0:T(8,128)(2,1)S(1)}, u32[]{:S(2)}, u32[]{:S(2)}) async-start(bf16[64,32,128]{2,1,0:T(8,128)(2,1)} %gate.1), calls=%async_computation | async-start | bytes 1048576 | tf_op jit(solution)/shard_map/all_to_all | solution.py:336
  15.3 0.0 copy-done.3
  15.3 0.7 %toeplitz.1.toep_ref = bf16[128,8320]{1,0:T(8,128)(2,1)S(1)} custom-call(f32[1,8192]{1,0:T(1,128)S(1)} %copy-done.3), custom_call_target="tpu_custom_call" | custom-call | tf_op jit(solution)/shard_map/toeplitz/pallas_call | solution.py:109
  16.0 15.7 %all-to-all-done.sig_ref = bf16[64,32,128]{2,1,0:T(8,128)(2,1)S(1)} async-done(((bf16[64,32,128]{2,1,0:T(8,128)(2,1)}), bf16[64,32,128]{2,1,0:T(8,128)(2,1)S(1)}, u32[]{:S(2)}, u32[]{:S(2)}) %all-to-all-start) | async-done | bytes 524320 | tf_op jit(solution)/shard_map/all_to_all | solution.py:336
  31.7 0.0 copy-done.4
  31.7 0.0 copy-start
  31.7 0.0 copy-start.1
  31.7 0.0 copy-start.2
  31.7 3.7 %conv.1 = bf16[64,32,128]{2,1,0:T(8,128)(2,1)} custom-call(bf16[64,32,128]{2,1,0:T(8,128)(2,1)S(1)} %all-to-all-done.sig_ref, bf16[128,8320]{1,0:T(8,128)(2,1)S(1)} %toeplitz.1.toep_ref, f32[8,128]{1,0:T(8,128)S(1)} %bitcast.16), custom_call_target="tpu_custom_call" | custom-call | tf_op jit(solution)/shard_map/conv/pallas_call | solution.py:183
  35.4 4.6 %all-to-all-start.1 = ((bf16[64,32,128]{2,1,0:T(8,128)(2,1)}), bf16[64,32,128]{2,1,0:T(8,128)(2,1)S(1)}, u32[]{:S(2)}, u32[]{:S(2)}) async-start(bf16[64,32,128]{2,1,0:T(8,128)(2,1)} %conv.1), calls=%async_computation.1 | async-start | bytes 1048576 | tf_op jit(solution)/shard_map/all_to_all | solution.py:338
  40.1 2.3 %cross.1 = f32[72,128]{1,0:T(8,128)S(1)} custom-call(bf16[64,32,128]{2,1,0:T(8,128)(2,1)S(1)} %all-to-all-done.sig_ref), custom_call_target="tpu_custom_call" | custom-call | tf_op jit(solution)/shard_map/cross/pallas_call | solution.py:242
  42.4 3.8 %all-gather = f32[144,128]{1,0:T(8,128)S(1)} all-gather(f32[72,128]{1,0:T(8,128)S(1)} %cross.1), channel_id=2, replica_groups={{0,64},{128,192},{256,320},{384,448},{1,65},{129,193},{257,321},{385,44..., dimensions={0}, use_global_device_ids=true | all-gather | bytes 110592 | tf_op jit(solution)/shard_map/all_gather | solution.py:343
  46.1 17.2 %all-reduce = (bf16[32,128]{1,0:T(8,128)(2,1)S(1)}, bf16[1,128]{1,0:T(2,128)(2,1)S(1)}) all-reduce(bf16[32,128]{1,0:T(8,128)(2,1)S(1)} %get-tuple-element.12, bf16[1,128]{1,0:T(2,128)(2,1)S(1)} %get-tuple-element.13), channel_id=1, replica_groups={{0,128,256,384},{64,192,320,448},{1,129,257,385},{65,193,321,449},{2,13..., use_global_device_ids=true, to_apply=%region_0.0 | all-reduce | flops 4224 | bytes 16896 | tf_op jit(solution)/shard_map/psum | solution.py:345
  63.3 3.6 %all_gather.11.sums_ref = bf16[64,128]{1,0:T(8,128)(2,1)S(1)} all-gather(bf16[32,128]{1,0:T(8,128)(2,1)S(1)} %get-tuple-element.19), channel_id=1, replica_groups={{0,64},{128,192},{256,320},{384,448},{1,65},{129,193},{257,321},{385,44..., dimensions={0}, use_global_device_ids=true | all-gather | bytes 24576 | tf_op jit(solution)/shard_map/all_gather | solution.py:346
  66.9 0.0 all-to-all-done.1.back_ref
  66.9 0.0 copy-done
  66.9 0.0 copy-done.1
  66.9 0.0 copy-done.2
  66.9 1.0 %final.1 = (bf16[64,16,128]{2,1,0:T(8,128)(2,1)}, bf16[64,16,128]{2,1,0:T(8,128)(2,1)}, bf16[64,16,128]{2,1,0:T(8,128)(2,1)}, f32[1,8192]{1,0:T(1,128)}, f32[16]{0:T(128)}) custom-call(bf16[64,32,128]{2,1,0:T(8,128)(2,1)S(1)} %all-to-all-done.1.back_ref, bf16[64,16,128]{2,1,0:T(8,128)(2,1)S(1)} %bitcast.10, bf16[64,16,128]{2,1,0:T(8,128)(2,1)S(1)} %bitcast.12, ...), custom_call_target="tpu_custom_call" | custom-call | tf_op jit(solution)/shard_map/final/pallas_call | solution.py:314
  (1 shorter events, 0.0 us)
Async XLA Ops:
  0.6 14.7 %copy-start.3 = (f32[1,8192]{1,0:T(1,128)S(1)}, f32[1,8192]{1,0:T(1,128)}, u32[]{:S(2)}) copy-start(f32[1,8192]{1,0:T(1,128)} %taps_ref.1) | copy-start | bytes 98308
  0.6 31.0 %copy-start.4 = (f32[1024]{0:T(1024)S(1)}, f32[1024]{0:T(1024)}, u32[]{:S(2)}) copy-start(f32[1024]{0:T(1024)} %param.11) | copy-start | bytes 12292
  2.8 28.8 %all-to-all-start = ((bf16[64,32,128]{2,1,0:T(8,128)(2,1)}), bf16[64,32,128]{2,1,0:T(8,128)(2,1)S(1)}, u32[]{:S(2)}, u32[]{:S(2)}) async-start(bf16[64,32,128]{2,1,0:T(8,128)(2,1)} %gate.1), calls=%async_computation | async-start | bytes 1048576 | tf_op jit(solution)/shard_map/all_to_all | solution.py:336
  31.7 35.2 %copy-start = (bf16[1,1024,128]{2,1,0:T(8,128)(2,1)S(1)}, bf16[1,1024,128]{2,1,0:T(8,128)(2,1)}, u32[]{:S(2)}) copy-start(bf16[1,1024,128]{2,1,0:T(8,128)(2,1)} %param.6) | copy-start | bytes 786436
  31.7 35.2 %copy-start.1 = (bf16[1,1024,128]{2,1,0:T(8,128)(2,1)S(1)}, bf16[1,1024,128]{2,1,0:T(8,128)(2,1)}, u32[]{:S(2)}) copy-start(bf16[1,1024,128]{2,1,0:T(8,128)(2,1)} %param.8) | copy-start | bytes 786436
  31.7 35.2 %copy-start.2 = (bf16[1,1024,128]{2,1,0:T(8,128)(2,1)S(1)}, bf16[1,1024,128]{2,1,0:T(8,128)(2,1)}, u32[]{:S(2)}) copy-start(bf16[1,1024,128]{2,1,0:T(8,128)(2,1)} %param.9) | copy-start | bytes 786436
  35.4 31.5 %all-to-all-start.1 = ((bf16[64,32,128]{2,1,0:T(8,128)(2,1)}), bf16[64,32,128]{2,1,0:T(8,128)(2,1)S(1)}, u32[]{:S(2)}, u32[]{:S(2)}) async-start(bf16[64,32,128]{2,1,0:T(8,128)(2,1)} %conv.1), calls=%async_computation.1 | async-start | bytes 1048576 | tf_op jit(solution)/shard_map/all_to_all | solution.py:338

commit v4 on v3

--- a/solution.py
+++ b/solution.py
@@ -11,10 +11,10 @@
 block = 256
 lag_group = 4
 mixed_order = (
-    17, 50, 1, 15, 12, 14, 30, 41, 37, 57, 60, 21, 35, 8, 61, 10,
-    22, 7, 44, 63, 46, 20, 55, 0, 31, 13, 58, 49, 19, 16, 25, 54,
-    36, 48, 52, 45, 34, 4, 26, 5, 3, 9, 51, 27, 24, 18, 38, 29,
-    43, 6, 33, 28, 23, 56, 2, 32, 40, 62, 47, 53, 42, 39, 59, 11,
+    17, 50, 1, 15, 12, 14, 30, 41, 37, 57, 60, 21, 35, 8, 61, 4,
+    22, 7, 44, 63, 46, 20, 55, 0, 31, 13, 58, 43, 19, 16, 25, 54,
+    36, 48, 52, 45, 34, 10, 26, 5, 3, 9, 2, 27, 28, 47, 38, 29,
+    49, 6, 33, 24, 23, 56, 51, 32, 40, 62, 18, 53, 42, 39, 59, 11,
 )
 whole = pl.BlockSpec(memory_space=pltpu.VMEM)
 gate_steps = 1

time: 68.3 us -> 68.4 us (level)
  no operation moved by 1% of the time
where the time goes in v4:
time: 68.4 us; the launch traced here: 68 us
  blocking collectives  24.8 us (36%)
  starting transfers between devices  16.8 us (25%)
  waiting for transfers between devices  15.8 us (23%)
  Pallas kernels  9.9 us (14%)
  between operations  0.72 us (1%)
    psum x1, blocking collectives, per_device(): half, bias = lax.psum((half, bias), 'dp', axis_index_groups=chips)  17.2 us
    all_to_all x1, waiting for transfers between devices, per_device(): lax.all_to_all(sent, 'seq', 0, 0, axis_index_groups=order, tiled=True)  15.8 us
    all_to_all x1, starting transfers between devices, per_device(): lax.all_to_all(sent, 'seq', 0, 0, axis_index_groups=order, tiled=True)  12.5 us
    all_to_all x1, starting transfers between devices, per_device(): lax.all_to_all(results, 'seq', 0, 0, axis_index_groups=order, tiled=True)  4.3 us
    all_gather x1, blocking collectives, per_device(): pair = lax.all_gather(partial, 'dp', axis_index_groups=cores)  3.89 us
    pallas_call x1, Pallas kernels, conv(): pl.pallas_call(conv_kernel, out_shape=jax.ShapeDtypeStruct(signals.shape,...  3.74 us
    all_gather x1, blocking collectives, per_device(): sums = lax.all_gather(half, 'dp', axis_index_groups=cores, tiled=True)  3.72 us
    pallas_call x1, Pallas kernels, cross(): pl.pallas_call(cross_kernel, out_shape=jax.ShapeDtypeStruct((parts + 8, l...  2.3 us
  transfers between devices with their start and end apart: 2, of which 1 were waited for; matrix products, arithmetic and copies ran while one was open for 0% of the time, Pallas kernels for 4%

profile of v4, /device:TPU:1, one launch (start us, length us, event | category | flops | bytes accessed | tf_op | source)
XLA Modules:
  0.0 68.0 jit_solution(17833930083772233111)
XLA Ops:
  0.6 0.0 copy-start.3
  0.6 0.0 copy-start.4
  0.7 2.2 %gate.1 = bf16[64,32,128]{2,1,0:T(8,128)(2,1)} custom-call(bf16[64,16,128]{2,1,0:T(8,128)(2,1)} %bitcast.9, bf16[64,16,128]{2,1,0:T(8,128)(2,1)} %bitcast.17, bf16[64,16,128]{2,1,0:T(8,128)(2,1)} %bitcast.11, bf16[64,16,128]{2,1,0:T(8,128)(2,1)} %bitcast.13), custom_call_target="tpu_custom_call" | custom-call | tf_op jit(solution)/shard_map/gate/pallas_call | solution.py:78
  2.8 12.5 %all-to-all-start = ((bf16[64,32,128]{2,1,0:T(8,128)(2,1)}), bf16[64,32,128]{2,1,0:T(8,128)(2,1)S(1)}, u32[]{:S(2)}, u32[]{:S(2)}) async-start(bf16[64,32,128]{2,1,0:T(8,128)(2,1)} %gate.1), calls=%async_computation | async-start | bytes 1048576 | tf_op jit(solution)/shard_map/all_to_all | solution.py:336
  15.3 0.0 copy-done.3
  15.3 0.7 %toeplitz.1.toep_ref = bf16[128,8320]{1,0:T(8,128)(2,1)S(1)} custom-call(f32[1,8192]{1,0:T(1,128)S(1)} %copy-done.3), custom_call_target="tpu_custom_call" | custom-call | tf_op jit(solution)/shard_map/toeplitz/pallas_call | solution.py:109
  16.0 15.8 %all-to-all-done.sig_ref = bf16[64,32,128]{2,1,0:T(8,128)(2,1)S(1)} async-done(((bf16[64,32,128]{2,1,0:T(8,128)(2,1)}), bf16[64,32,128]{2,1,0:T(8,128)(2,1)S(1)}, u32[]{:S(2)}, u32[]{:S(2)}) %all-to-all-start) | async-done | bytes 524320 | tf_op jit(solution)/shard_map/all_to_all | solution.py:336
  31.8 0.0 copy-done.4
  31.8 0.0 copy-start
  31.8 0.0 copy-start.1
  31.8 0.0 copy-start.2
  31.8 3.7 %conv.1 = bf16[64,32,128]{2,1,0:T(8,128)(2,1)} custom-call(bf16[64,32,128]{2,1,0:T(8,128)(2,1)S(1)} %all-to-all-done.sig_ref, bf16[128,8320]{1,0:T(8,128)(2,1)S(1)} %toeplitz.1.toep_ref, f32[8,128]{1,0:T(8,128)S(1)} %bitcast.16), custom_call_target="tpu_custom_call" | custom-call | tf_op jit(solution)/shard_map/conv/pallas_call | solution.py:183
  35.6 4.3 %all-to-all-start.1 = ((bf16[64,32,128]{2,1,0:T(8,128)(2,1)}), bf16[64,32,128]{2,1,0:T(8,128)(2,1)S(1)}, u32[]{:S(2)}, u32[]{:S(2)}) async-start(bf16[64,32,128]{2,1,0:T(8,128)(2,1)} %conv.1), calls=%async_computation.1 | async-start | bytes 1048576 | tf_op jit(solution)/shard_map/all_to_all | solution.py:338
  39.9 2.3 %cross.1 = f32[72,128]{1,0:T(8,128)S(1)} custom-call(bf16[64,32,128]{2,1,0:T(8,128)(2,1)S(1)} %all-to-all-done.sig_ref), custom_call_target="tpu_custom_call" | custom-call | tf_op jit(solution)/shard_map/cross/pallas_call | solution.py:242
  42.2 3.9 %all-gather = f32[144,128]{1,0:T(8,128)S(1)} all-gather(f32[72,128]{1,0:T(8,128)S(1)} %cross.1), channel_id=2, replica_groups={{0,64},{128,192},{256,320},{384,448},{1,65},{129,193},{257,321},{385,44..., dimensions={0}, use_global_device_ids=true | all-gather | bytes 110592 | tf_op jit(solution)/shard_map/all_gather | solution.py:343
  46.1 17.2 %all-reduce = (bf16[32,128]{1,0:T(8,128)(2,1)S(1)}, bf16[1,128]{1,0:T(2,128)(2,1)S(1)}) all-reduce(bf16[32,128]{1,0:T(8,128)(2,1)S(1)} %get-tuple-element.12, bf16[1,128]{1,0:T(2,128)(2,1)S(1)} %get-tuple-element.13), channel_id=1, replica_groups={{0,128,256,384},{64,192,320,448},{1,129,257,385},{65,193,321,449},{2,13..., use_global_device_ids=true, to_apply=%region_0.0 | all-reduce | flops 4224 | bytes 16896 | tf_op jit(solution)/shard_map/psum | solution.py:345
  63.3 3.7 %all_gather.11.sums_ref = bf16[64,128]{1,0:T(8,128)(2,1)S(1)} all-gather(bf16[32,128]{1,0:T(8,128)(2,1)S(1)} %get-tuple-element.19), channel_id=1, replica_groups={{0,64},{128,192},{256,320},{384,448},{1,65},{129,193},{257,321},{385,44..., dimensions={0}, use_global_device_ids=true | all-gather | bytes 24576 | tf_op jit(solution)/shard_map/all_gather | solution.py:346
  67.0 0.0 all-to-all-done.1.back_ref
  67.0 0.0 copy-done
  67.0 0.0 copy-done.1
  67.0 0.0 copy-done.2
  67.0 1.0 %final.1 = (bf16[64,16,128]{2,1,0:T(8,128)(2,1)}, bf16[64,16,128]{2,1,0:T(8,128)(2,1)}, bf16[64,16,128]{2,1,0:T(8,128)(2,1)}, f32[1,8192]{1,0:T(1,128)}, f32[16]{0:T(128)}) custom-call(bf16[64,32,128]{2,1,0:T(8,128)(2,1)S(1)} %all-to-all-done.1.back_ref, bf16[64,16,128]{2,1,0:T(8,128)(2,1)S(1)} %bitcast.10, bf16[64,16,128]{2,1,0:T(8,128)(2,1)S(1)} %bitcast.12, ...), custom_call_target="tpu_custom_call" | custom-call | tf_op jit(solution)/shard_map/final/pallas_call | solution.py:314
  (1 shorter events, 0.0 us)
Async XLA Ops:
  0.6 14.7 %copy-start.3 = (f32[1,8192]{1,0:T(1,128)S(1)}, f32[1,8192]{1,0:T(1,128)}, u32[]{:S(2)}) copy-start(f32[1,8192]{1,0:T(1,128)} %taps_ref.1) | copy-start | bytes 98308
  0.6 31.2 %copy-start.4 = (f32[1024]{0:T(1024)S(1)}, f32[1024]{0:T(1024)}, u32[]{:S(2)}) copy-start(f32[1024]{0:T(1024)} %param.11) | copy-start | bytes 12292
  2.8 29.0 %all-to-all-start = ((bf16[64,32,128]{2,1,0:T(8,128)(2,1)}), bf16[64,32,128]{2,1,0:T(8,128)(2,1)S(1)}, u32[]{:S(2)}, u32[]{:S(2)}) async-start(bf16[64,32,128]{2,1,0:T(8,128)(2,1)} %gate.1), calls=%async_computation | async-start | bytes 1048576 | tf_op jit(solution)/shard_map/all_to_all | solution.py:336
  31.8 35.2 %copy-start = (bf16[1,1024,128]{2,1,0:T(8,128)(2,1)S(1)}, bf16[1,1024,128]{2,1,0:T(8,128)(2,1)}, u32[]{:S(2)}) copy-start(bf16[1,1024,128]{2,1,0:T(8,128)(2,1)} %param.6) | copy-start | bytes 786436
  31.8 35.2 %copy-start.1 = (bf16[1,1024,128]{2,1,0:T(8,128)(2,1)S(1)}, bf16[1,1024,128]{2,1,0:T(8,128)(2,1)}, u32[]{:S(2)}) copy-start(bf16[1,1024,128]{2,1,0:T(8,128)(2,1)} %param.8) | copy-start | bytes 786436
  31.8 35.2 %copy-start.2 = (bf16[1,1024,128]{2,1,0:T(8,128)(2,1)S(1)}, bf16[1,1024,128]{2,1,0:T(8,128)(2,1)}, u32[]{:S(2)}) copy-start(bf16[1,1024,128]{2,1,0:T(8,128)(2,1)} %param.9) | copy-start | bytes 786436
  35.6 31.4 %all-to-all-start.1 = ((bf16[64,32,128]{2,1,0:T(8,128)(2,1)}), bf16[64,32,128]{2,1,0:T(8,128)(2,1)S(1)}, u32[]{:S(2)}, u32[]{:S(2)}) async-start(bf16[64,32,128]{2,1,0:T(8,128)(2,1)} %conv.1), calls=%async_computation.1 | async-start | bytes 1048576 | tf_op jit(solution)/shard_map/all_to_all | solution.py:338
